TPU v7x, 32 devices: a whole 2x2x4 slice. The times are simulated.
32 devices in a mesh: leaf: 32 (over z, y, x, core).
Axes of the slice: x: 2, y: 2, z: 4, core: 2. Of those that a mesh axis runs over, the one named last changes fastest.
Arguments:
- right_side: float32 [16, 131072], P(None, 'leaf'), may hold values from -12 to 12
- basis: bfloat16 [512, 64, 256], P('leaf'), may hold values from -0.5 to 0.5
- transfer: bfloat16 [960, 64, 64], P('leaf'), may hold values from -0.5 to 0.5
- near_tiles: bfloat16 [512, 8, 256, 256], P('leaf'), may hold values from -4 to 4
- near_source: int32 [512, 8], P('leaf'), may hold values from 0 to 511, as said below
- near_count: int32 [512], P('leaf'), may hold values from 1 to 8, as said below
- couple: bfloat16 [448, 6, 64, 64], P('leaf'), may hold values from -1.5 to 1.5
- couple_source: int32 [448, 6], P('leaf'), may hold values from 0 to 255, as said below
- couple_count: int32 [448], P('leaf'), may hold values from 1 to 6, as said below
- root_couple: bfloat16 [32, 5, 64, 64], P('leaf'), may hold values from -4 to 4
- root_mask: int32 [32, 5], P('leaf'), may hold values 0 or 1
Outputs:
- solution: float32 [16, 131072], P(None, 'leaf')
- residual: float32 [16, 131072], P(None, 'leaf')
Inputs may be any that keep to these rules, and one draw needn't show every extreme that they name: `near_source`: slot 0 of leaf g is g itself; every slot names a different leaf of the same subtree or of one of the two subtrees beside it. `near_count`: the live tiles are the first slots; on each subtree some leaf has the most live tiles of that subtree. `couple_source`: a source is a cluster of the same level, not the cluster itself, in the same subtree or in one of the two subtrees beside it. `couple_count`: the live blocks are the first slots.
All inputs are finite; a program needn't handle non-finite values. No bound on the sum of `root_mask` on one device may be relied on, other than what follows from the above.
Results may differ from a plain program's by a relative error of at most 0.014.
Values may be sent and summed in bfloat16 or wider, within the bound.
A program may use at most 128 MiB of HBM per device.

v0:
```python
import functools

import jax
import jax.numpy as jnp
from jax import lax
from jax.experimental import pallas as pl
from jax.experimental.pallas import tpu as pltpu
from jax.sharding import PartitionSpec as P

MESH = pl.DeviceIdType.MESH
F32 = jnp.float32
BF16 = jnp.bfloat16
SHRINK = 2.0**-10
GROW = 2.0**10
UNROLL = 4


def dot(a, b):
    return jnp.dot(a, b, preferred_element_type=F32)


def dot_t(a, b):
    return lax.dot_general(a, b, (((1,), (1,)), ((), ())), preferred_element_type=F32)


def level_sizes(leaf_dev):
    sizes = [leaf_dev]
    while sizes[-1] > 1:
        sizes.append(sizes[-1] // 2)
    return sizes


def kernel(
    count,
    near_source,
    near_count,
    couple_source,
    couple_count,
    root_mask,
    rhs_hbm,
    basis_hbm,
    transfer_hbm,
    near_hbm,
    couple_hbm,
    root_hbm,
    sol_ref,
    res_ref,
    rhs,
    basis,
    transfer,
    near,
    couple,
    root,
    image_a,
    image_b,
    field0,
    win_a,
    win_b,
    cwin_a,
    cwin_b,
    own_a,
    own_b,
    part_a,
    part_b,
    red_a,
    red_b,
    load_sem,
    near_sem,
    halo_send,
    halo_recv,
    coef_send,
    coef_recv,
    root_send,
    root_recv,
    red_send,
    red_recv,
):
    leaf_dev, rank, leaf = basis.shape
    slots = near.shape[1]
    nrhs = rhs.shape[0]
    bits = root.shape[0]
    sizes = level_sizes(leaf_dev)
    top = len(sizes) - 1
    starts = [sum(sizes[:level]) for level in range(top)]
    me = lax.axis_index("leaf")
    has_left = me > 0
    has_right = me < count - 1

    loads = [
        pltpu.make_async_copy(src, dst, load_sem.at[i])
        for i, (src, dst) in enumerate(
            (
                (rhs_hbm, rhs),
                (basis_hbm, basis),
                (transfer_hbm, transfer),
                (couple_hbm, couple),
                (root_hbm, root),
            )
        )
    ]
    for load in loads:
        load.start()

    def near_load(g):
        return pltpu.make_async_copy(near_hbm.at[g], near.at[g], near_sem.at[g])

    for g in range(leaf_dev):
        near_load(g).start()

    barrier = pltpu.get_barrier_semaphore()

    def greet(k, carry):
        pl.semaphore_signal(
            barrier, inc=1, device_id=(lax.rem(me + k, count),), device_id_type=MESH
        )
        return carry

    lax.fori_loop(1, count, greet, 0)

    def halo_copies(it, win):
        own = win.at[pl.ds(leaf_dev, leaf_dev)]
        to_right = pltpu.make_async_remote_copy(
            src_ref=own,
            dst_ref=win.at[pl.ds(0, leaf_dev)],
            send_sem=halo_send.at[it, 0],
            recv_sem=halo_recv.at[it, 0],
            device_id=(me + 1,),
            device_id_type=MESH,
        )
        to_left = pltpu.make_async_remote_copy(
            src_ref=own,
            dst_ref=win.at[pl.ds(2 * leaf_dev, leaf_dev)],
            send_sem=halo_send.at[it, 1],
            recv_sem=halo_recv.at[it, 1],
            device_id=(me - 1,),
            device_id_type=MESH,
        )
        return to_right, to_left

    def coef_copies(it, level, cwin):
        size = sizes[level]
        own = cwin.at[pl.ds(size, size)]
        to_right = pltpu.make_async_remote_copy(
            src_ref=own,
            dst_ref=cwin.at[pl.ds(0, size)],
            send_sem=coef_send.at[it, level - 1, 0],
            recv_sem=coef_recv.at[it, level - 1, 0],
            device_id=(me + 1,),
            device_id_type=MESH,
        )
        to_left = pltpu.make_async_remote_copy(
            src_ref=own,
            dst_ref=cwin.at[pl.ds(2 * size, size)],
            send_sem=coef_send.at[it, level - 1, 1],
            recv_sem=coef_recv.at[it, level - 1, 1],
            device_id=(me - 1,),
            device_id_type=MESH,
        )
        return to_right, to_left

    def start_pair(pair):
        to_right, to_left = pair

        @pl.when(has_right)
        def _():
            to_right.start()

        @pl.when(has_left)
        def _():
            to_left.start()

    def recv_pair(pair):
        to_right, to_left = pair

        @pl.when(has_left)
        def _():
            to_right.wait_recv()

        @pl.when(has_right)
        def _():
            to_left.wait_recv()

    def sent_pair(pair):
        to_right, to_left = pair

        @pl.when(has_right)
        def _():
            to_right.wait_send()

        @pl.when(has_left)
        def _():
            to_left.wait_send()

    def root_copy(it, bit, own):
        step = 1 << bit
        partner = me + step * (1 - 2 * lax.rem(me // step, 2))
        return pltpu.make_async_remote_copy(
            src_ref=own.at[0],
            dst_ref=own.at[1 + bit],
            send_sem=root_send.at[it, bit],
            recv_sem=root_recv.at[it, bit],
            device_id=(partner,),
            device_id_type=MESH,
        )

    def upward(it, win, cwins, own):
        coef = [
            dot_t(win[leaf_dev + g], basis[g]).astype(BF16) for g in range(leaf_dev)
        ]
        for level in range(1, top + 1):
            at = starts[level - 1]
            raised = []
            for j in range(sizes[level]):
                raised.append(
                    (
                        dot(coef[2 * j], transfer[at + 2 * j])
                        + dot(coef[2 * j + 1], transfer[at + 2 * j + 1])
                    ).astype(BF16)
                )
            coef = raised
            if level < top:
                cwin = cwins[level - 1]
                for j in range(sizes[level]):
                    cwin[sizes[level] + j] = coef[j]
                start_pair(coef_copies(it, level, cwin))
        own[0] = coef[0]
        for bit in range(bits):
            root_copy(it, bit, own).start()

    def downward(it, cwins, own):
        for level in range(1, top):
            recv_pair(coef_copies(it, level, cwins[level - 1]))
        for bit in range(bits):
            root_copy(it, bit, own).wait_recv()
        total = jnp.zeros((nrhs, rank), F32)
        for bit in range(bits):
            total = total + root_mask[0, bit].astype(F32) * dot(own[1 + bit], root[bit])
        field = [total.astype(BF16)]
        for level in range(top - 1, -1, -1):
            down = []
            for j in range(sizes[level]):
                value = dot_t(field[j // 2], transfer[starts[level] + j])
                if level >= 1:
                    row = starts[level] - sizes[0] + j
                    live_slots = couple_count[row]
                    for s in range(couple.shape[1]):
                        index = couple_source[s, row] - (me - 1) * sizes[level]
                        index = jnp.clip(index, 0, 3 * sizes[level] - 1)
                        live = (s < live_slots).astype(F32)
                        value = value + live * dot(
                            cwins[level - 1][index], couple[row, s]
                        )
                down.append(value.astype(BF16))
            field = down
        for g in range(leaf_dev):
            field0[g] = field[g]

    def leaves(it, win, image, wait):
        base = (me - 1) * leaf_dev

        def step(i, carry):
            if wait:
                for u in range(UNROLL):
                    near_load(i * UNROLL + u).wait()
            for u in range(UNROLL):
                g = i * UNROLL + u
                live_slots = near_count[g]
                picked = []
                for s in range(slots):
                    live = (s < live_slots).astype(F32).astype(BF16)
                    index = jnp.clip(near_source[s, g] - base, 0, 3 * leaf_dev - 1)
                    picked.append(win[index] * live)
                x = jnp.concatenate(picked, axis=1)
                tile = near[g].reshape(slots * leaf, leaf)
                block = dot(x, tile) + dot(field0[g], basis[g])
                image[:, pl.ds(pl.multiple_of(g * leaf, leaf), leaf)] = block
            return carry

        lax.fori_loop(0, leaf_dev // UNROLL, step, 0)

    rows = lax.broadcasted_iota(jnp.int32, (nrhs, 128), 0)
    lanes = lax.broadcasted_iota(jnp.int32, (nrhs, 128), 1)

    def red_copy(it, k, part, red):
        return pltpu.make_async_remote_copy(
            src_ref=part,
            dst_ref=red.at[me],
            send_sem=red_send.at[it, k],
            recv_sem=red_recv.at[it, k],
            device_id=(lax.rem(me + k, count),),
            device_id_type=MESH,
        )

    def reduce_start(it, first, second, part, red):
        upper = jnp.sum(first * second, axis=1, keepdims=True)
        lower = jnp.sum(second * second, axis=1, keepdims=True)
        both = jnp.where(lanes == rows, upper, 0.0) + jnp.where(
            lanes == rows + nrhs, lower, 0.0
        )
        row = jnp.sum(both, axis=0, keepdims=True)
        part[...] = row
        red[me] = row

        def send(k, carry):
            red_copy(it, k, part, red).start()
            return carry

        lax.fori_loop(1, count, send, 0)

    def reduce_end(it, part, red):
        def take(k, carry):
            red_copy(it, k, part, red).wait_recv()
            return carry

        lax.fori_loop(1, count, take, 0)
        total = jnp.sum(red[...], axis=0)
        wide = jnp.broadcast_to(total, (nrhs, 128))
        upper = jnp.sum(jnp.where(lanes == rows, wide, 0.0), axis=1, keepdims=True)
        lower = jnp.sum(
            jnp.where(lanes == rows + nrhs, wide, 0.0), axis=1, keepdims=True
        )
        return upper / (lower + 1e-06)

    def to_window(win, source, scale):
        for g in range(leaf_dev):
            block = source[:, g * leaf : (g + 1) * leaf]
            if scale is not None:
                block = block * scale
            win[leaf_dev + g] = block.astype(BF16)

    loads[0].wait()
    to_window(win_a, rhs, None)
    pl.semaphore_wait(barrier, count - 1)
    start_pair(halo_copies(0, win_a))
    for load in loads[1:]:
        load.wait()
    upward(0, win_a, cwin_a, own_a)
    downward(0, cwin_a, own_a)
    recv_pair(halo_copies(0, win_a))
    leaves(0, win_a, image_a, True)

    to_window(win_b, image_a, SHRINK)
    start_pair(halo_copies(1, win_b))
    reduce_start(0, rhs[...], image_a[...], part_a, red_a)
    upward(1, win_b, cwin_b, own_b)
    downward(1, cwin_b, own_b)
    recv_pair(halo_copies(1, win_b))
    leaves(1, win_b, image_b, False)

    alpha = reduce_end(0, part_a, red_a)
    residual = rhs[...] - alpha * image_a[...]
    image = image_a[...] - (alpha * GROW) * image_b[...]
    reduce_start(1, residual, image, part_b, red_b)
    res_ref[...] = residual
    image_b[...] = image

    for it, win, cwins, own, part, red in (
        (0, win_a, cwin_a, own_a, part_a, red_a),
        (1, win_b, cwin_b, own_b, part_b, red_b),
    ):
        sent_pair(halo_copies(it, win))
        for level in range(1, top):
            sent_pair(coef_copies(it, level, cwins[level - 1]))
        for bit in range(bits):
            root_copy(it, bit, own).wait_send()

    beta = reduce_end(1, part_b, red_b)
    sol_ref[...] = alpha * rhs[...] + beta * res_ref[...]
    res_ref[...] = res_ref[...] - beta * image_b[...]

    def drain(k, carry):
        red_copy(0, k, part_a, red_a).wait_send()
        red_copy(1, k, part_b, red_b).wait_send()
        return carry

    lax.fori_loop(1, count, drain, 0)


def body(
    count,
    right_side,
    basis,
    transfer,
    near_tiles,
    near_source,
    near_count,
    couple,
    couple_source,
    couple_count,
    root_couple,
    root_mask,
):
    leaf_dev, rank, leaf = basis.shape
    nrhs = right_side.shape[0]
    sizes = level_sizes(leaf_dev)
    top = len(sizes) - 1
    bits = root_couple.shape[1]
    root_couple = root_couple.reshape(root_couple.shape[1:])
    smem = pl.BlockSpec(memory_space=pltpu.SMEM)
    hbm = pl.BlockSpec(memory_space=pl.ANY)
    vmem = pl.BlockSpec(memory_space=pltpu.VMEM)
    cwins = [pltpu.VMEM((3 * sizes[level], nrhs, rank), BF16) for level in range(1, top)]
    dma = pltpu.SemaphoreType.DMA
    out = jax.ShapeDtypeStruct(right_side.shape, F32)
    return pl.pallas_call(
        functools.partial(kernel, count),
        out_shape=(out, out),
        in_specs=[smem] * 5 + [hbm] * 6,
        out_specs=(vmem, vmem),
        scratch_shapes=[
            pltpu.VMEM(right_side.shape, F32),
            pltpu.VMEM(basis.shape, BF16),
            pltpu.VMEM(transfer.shape, BF16),
            pltpu.VMEM(near_tiles.shape, BF16),
            pltpu.VMEM(couple.shape, BF16),
            pltpu.VMEM(root_couple.shape, BF16),
            pltpu.VMEM(right_side.shape, F32),
            pltpu.VMEM(right_side.shape, F32),
            pltpu.VMEM((leaf_dev, nrhs, rank), BF16),
            pltpu.VMEM((3 * leaf_dev, nrhs, leaf), BF16),
            pltpu.VMEM((3 * leaf_dev, nrhs, leaf), BF16),
            cwins,
            cwins,
            pltpu.VMEM((1 + bits, nrhs, rank), BF16),
            pltpu.VMEM((1 + bits, nrhs, rank), BF16),
            pltpu.VMEM((1, 128), F32),
            pltpu.VMEM((1, 128), F32),
            pltpu.VMEM((count, 1, 128), F32),
            pltpu.VMEM((count, 1, 128), F32),
            dma((5,)),
            dma((leaf_dev,)),
            dma((2, 2)),
            dma((2, 2)),
            dma((2, top - 1, 2)),
            dma((2, top - 1, 2)),
            dma((2, bits)),
            dma((2, bits)),
            dma((2, count)),
            dma((2, count)),
        ],
        compiler_params=pltpu.CompilerParams(
            collective_id=0, has_side_effects=True, vmem_limit_bytes=56 << 20
        ),
        cost_estimate=pl.CostEstimate(
            flops=4 * nrhs * near_tiles.size,
            bytes_accessed=2 * near_tiles.size,
            transcendentals=0,
        ),
    )(
        near_source.T,
        near_count,
        couple_source.T,
        couple_count,
        root_mask,
        right_side,
        basis,
        transfer,
        near_tiles,
        couple,
        root_couple,
    )


def solution(mesh):
    in_specs = (
        P(None, "leaf"),
        P("leaf", None, None),
        P("leaf", None, None),
        P("leaf", None, None, None),
        P("leaf", None),
        P("leaf"),
        P("leaf", None, None, None),
        P("leaf", None),
        P("leaf"),
        P("leaf", None, None, None),
        P("leaf", None),
    )
    out_specs = (P(None, "leaf"), P(None, "leaf"))
    return jax.shard_map(
        functools.partial(body, mesh.shape["leaf"]),
        mesh=mesh,
        in_specs=in_specs,
        out_specs=out_specs,
        check_vma=False,
    )
```

profile of v0, /device:TPU:0, one launch (start us, length us, event | category | flops | bytes accessed | tf_op | source)
XLA Modules:
  0.0 40.3 jit_solution(8423027722773853868)
XLA Ops:
  0.6 36.3 %shard_map.122 = (f32[16,4096]{1,0:T(8,128)}, f32[16,4096]{1,0:T(8,128)}) custom-call(s32[8,16]{1,0:T(8,128)} %bitcast.4, s32[16]{0:T(128)} %near_count.1, s32[6,14]{1,0:T(8,128)} %bitcast.5, s32[14]{0:T(128)} %couple_count.1, s32[1,5]{1,0:T(1,128)} %root_mask.1, f32[16,4096]{1,0:T(8,128)} %rhs_hbm.1, bf16[16,64,256]{2,1,0:T(8,128)(2,1)} %basis_hbm.1, ...), custom_call_target="tpu_custom_call" | custom-call | flops 536870912 | bytes 16777216 | tf_op jit(solution)/shard_map/pallas_call | solution.py:405
  36.9 1.7 %copy.15 = f32[16,4096]{1,0:T(8,128)} copy(f32[16,4096]{1,0:T(8,128)} %get-tuple-element.4) | data formatting | bytes 524288
  38.6 1.7 %copy.16 = f32[16,4096]{1,0:T(8,128)} copy(f32[16,4096]{1,0:T(8,128)} %get-tuple-element.5) | data formatting | bytes 524288
where the time goes:
time: 40.5 us; the launch traced here: 40.3 us
  Pallas kernels  36.3 us (90%)
  local copies, waits for them, and re-layouts  3.34 us (8%)
  between operations  0.64 us (2%)
    pallas_call x1, Pallas kernels, body(): pl.pallas_call(functools.partial(kernel, count), out_shape=(out, out), in...  36.3 us
    unnamed x2, local copies, waits for them, and re-layouts  3.34 us

commit v1 on v0

--- a/solution.py
+++ b/solution.py
@@ -32,19 +32,26 @@
 
 def kernel(
     count,
-    near_source,
-    near_count,
-    couple_source,
-    couple_count,
-    root_mask,
+    near_source_hbm,
+    near_count_hbm,
+    couple_source_hbm,
+    couple_count_hbm,
+    root_mask_hbm,
     rhs_hbm,
     basis_hbm,
     transfer_hbm,
     near_hbm,
     couple_hbm,
     root_hbm,
-    sol_ref,
-    res_ref,
+    residual_hbm,
+    image_hbm,
+    alpha_ref,
+    beta_ref,
+    near_source,
+    near_count,
+    couple_source,
+    couple_count,
+    root_mask,
     rhs,
     basis,
     transfer,
@@ -53,7 +60,8 @@
     root,
     image_a,
     image_b,
-    field0,
+    residual,
+    coupled,
     win_a,
     win_b,
     cwin_a,
@@ -66,6 +74,7 @@
     red_b,
     load_sem,
     near_sem,
+    out_sem,
     halo_send,
     halo_recv,
     coef_send,
@@ -95,6 +104,11 @@
                 (transfer_hbm, transfer),
                 (couple_hbm, couple),
                 (root_hbm, root),
+                (near_source_hbm, near_source),
+                (near_count_hbm, near_count),
+                (couple_source_hbm, couple_source),
+                (couple_count_hbm, couple_count),
+                (root_mask_hbm, root_mask),
             )
         )
     ]
@@ -103,9 +117,6 @@
 
     def near_load(g):
         return pltpu.make_async_copy(near_hbm.at[g], near.at[g], near_sem.at[g])
-
-    for g in range(leaf_dev):
-        near_load(g).start()
 
     barrier = pltpu.get_barrier_semaphore()
 
@@ -227,9 +238,50 @@
         for bit in range(bits):
             root_copy(it, bit, own).start()
 
-    def downward(it, cwins, own):
+    def couplings(it, cwins):
         for level in range(1, top):
             recv_pair(coef_copies(it, level, cwins[level - 1]))
+        for level in range(1, top):
+            for j in range(sizes[level]):
+                row = starts[level] - sizes[0] + j
+                live_slots = couple_count[row]
+                value = jnp.zeros((nrhs, rank), F32)
+                for s in range(couple.shape[1]):
+                    index = couple_source[s, row] - (me - 1) * sizes[level]
+                    index = jnp.clip(index, 0, 3 * sizes[level] - 1)
+                    live = (s < live_slots).astype(F32)
+                    value = value + live * dot(cwins[level - 1][index], couple[row, s])
+                coupled[row] = value
+
+    def near_field(g, win):
+        base = (me - 1) * leaf_dev
+        live_slots = near_count[g]
+        picked = []
+        for s in range(slots):
+            live = (s < live_slots).astype(F32).astype(BF16)
+            index = jnp.clip(near_source[s, g] - base, 0, 3 * leaf_dev - 1)
+            picked.append(win[index] * live)
+        x = jnp.concatenate(picked, axis=1)
+        return dot(x, near[g].reshape(slots * leaf, leaf))
+
+    def early_leaves(win, image, wait):
+        def step(i, carry):
+            if wait:
+                for u in range(UNROLL):
+                    near_load(i * UNROLL + u).wait()
+            for u in range(UNROLL):
+                g = i * UNROLL + u
+                lane = pl.ds(pl.multiple_of(g * leaf, leaf), leaf)
+                image[:, lane] = near_field(g, win)
+            return carry
+
+        lax.fori_loop(0, leaf_dev // UNROLL - 1, step, 0)
+
+    def late_leaves(it, win, own, image, following, wait):
+        last = leaf_dev - UNROLL
+        if wait:
+            for g in range(last, leaf_dev):
+                near_load(g).wait()
         for bit in range(bits):
             root_copy(it, bit, own).wait_recv()
         total = jnp.zeros((nrhs, rank), F32)
@@ -241,42 +293,17 @@
             for j in range(sizes[level]):
                 value = dot_t(field[j // 2], transfer[starts[level] + j])
                 if level >= 1:
-                    row = starts[level] - sizes[0] + j
-                    live_slots = couple_count[row]
-                    for s in range(couple.shape[1]):
-                        index = couple_source[s, row] - (me - 1) * sizes[level]
-                        index = jnp.clip(index, 0, 3 * sizes[level] - 1)
-                        live = (s < live_slots).astype(F32)
-                        value = value + live * dot(
-                            cwins[level - 1][index], couple[row, s]
-                        )
+                    value = value + coupled[starts[level] - sizes[0] + j]
                 down.append(value.astype(BF16))
             field = down
+        late = [near_field(g, win) for g in range(last, leaf_dev)]
         for g in range(leaf_dev):
-            field0[g] = field[g]
-
-    def leaves(it, win, image, wait):
-        base = (me - 1) * leaf_dev
-
-        def step(i, carry):
-            if wait:
-                for u in range(UNROLL):
-                    near_load(i * UNROLL + u).wait()
-            for u in range(UNROLL):
-                g = i * UNROLL + u
-                live_slots = near_count[g]
-                picked = []
-                for s in range(slots):
-                    live = (s < live_slots).astype(F32).astype(BF16)
-                    index = jnp.clip(near_source[s, g] - base, 0, 3 * leaf_dev - 1)
-                    picked.append(win[index] * live)
-                x = jnp.concatenate(picked, axis=1)
-                tile = near[g].reshape(slots * leaf, leaf)
-                block = dot(x, tile) + dot(field0[g], basis[g])
-                image[:, pl.ds(pl.multiple_of(g * leaf, leaf), leaf)] = block
-            return carry
-
-        lax.fori_loop(0, leaf_dev // UNROLL, step, 0)
+            lane = slice(g * leaf, (g + 1) * leaf)
+            block = image[:, lane] if g < last else late[g - last]
+            block = block + dot(field[g], basis[g])
+            image[:, lane] = block
+            if following is not None:
+                following[leaf_dev + g] = (block * SHRINK).astype(BF16)
 
     rows = lax.broadcasted_iota(jnp.int32, (nrhs, 128), 0)
     lanes = lax.broadcasted_iota(jnp.int32, (nrhs, 128), 1)
@@ -285,11 +312,15 @@
         return pltpu.make_async_remote_copy(
             src_ref=part,
             dst_ref=red.at[me],
-            send_sem=red_send.at[it, k],
-            recv_sem=red_recv.at[it, k],
+            send_sem=red_send.at[it],
+            recv_sem=red_recv.at[it],
             device_id=(lax.rem(me + k, count),),
             device_id_type=MESH,
         )
+
+    def every_row(red, sem):
+        rows_of_others = red.at[pl.ds(0, count - 1)]
+        return pltpu.make_async_copy(rows_of_others, rows_of_others, sem)
 
     def reduce_start(it, first, second, part, red):
         upper = jnp.sum(first * second, axis=1, keepdims=True)
@@ -308,11 +339,7 @@
         lax.fori_loop(1, count, send, 0)
 
     def reduce_end(it, part, red):
-        def take(k, carry):
-            red_copy(it, k, part, red).wait_recv()
-            return carry
-
-        lax.fori_loop(1, count, take, 0)
+        every_row(red, red_recv.at[it]).wait()
         total = jnp.sum(red[...], axis=0)
         wide = jnp.broadcast_to(total, (nrhs, 128))
         upper = jnp.sum(jnp.where(lanes == rows, wide, 0.0), axis=1, keepdims=True)
@@ -321,59 +348,57 @@
         )
         return upper / (lower + 1e-06)
 
-    def to_window(win, source, scale):
-        for g in range(leaf_dev):
-            block = source[:, g * leaf : (g + 1) * leaf]
-            if scale is not None:
-                block = block * scale
-            win[leaf_dev + g] = block.astype(BF16)
-
     loads[0].wait()
-    to_window(win_a, rhs, None)
+    for g in range(leaf_dev):
+        win_a[leaf_dev + g] = rhs[:, g * leaf : (g + 1) * leaf].astype(BF16)
     pl.semaphore_wait(barrier, count - 1)
     start_pair(halo_copies(0, win_a))
-    for load in loads[1:]:
+    for load in loads[1:3]:
         load.wait()
+    for g in range(leaf_dev):
+        near_load(g).start()
     upward(0, win_a, cwin_a, own_a)
-    downward(0, cwin_a, own_a)
+    for load in loads[3:]:
+        load.wait()
+    couplings(0, cwin_a)
     recv_pair(halo_copies(0, win_a))
-    leaves(0, win_a, image_a, True)
-
-    to_window(win_b, image_a, SHRINK)
+    early_leaves(win_a, image_a, True)
+    late_leaves(0, win_a, own_a, image_a, win_b, True)
+
     start_pair(halo_copies(1, win_b))
     reduce_start(0, rhs[...], image_a[...], part_a, red_a)
     upward(1, win_b, cwin_b, own_b)
-    downward(1, cwin_b, own_b)
+    couplings(1, cwin_b)
     recv_pair(halo_copies(1, win_b))
-    leaves(1, win_b, image_b, False)
-
+    early_leaves(win_b, image_b, False)
     alpha = reduce_end(0, part_a, red_a)
-    residual = rhs[...] - alpha * image_a[...]
-    image = image_a[...] - (alpha * GROW) * image_b[...]
-    reduce_start(1, residual, image, part_b, red_b)
-    res_ref[...] = residual
-    image_b[...] = image
-
-    for it, win, cwins, own, part, red in (
-        (0, win_a, cwin_a, own_a, part_a, red_a),
-        (1, win_b, cwin_b, own_b, part_b, red_b),
+    alpha_ref[...] = jnp.broadcast_to(alpha, alpha_ref.shape)
+    residual[...] = rhs[...] - alpha * image_a[...]
+    residual_out = pltpu.make_async_copy(residual, residual_hbm, out_sem.at[0])
+    residual_out.start()
+    late_leaves(1, win_b, own_b, image_b, None, False)
+
+    alpha = alpha_ref[:, :1]
+    image_b[...] = image_a[...] - (alpha * GROW) * image_b[...]
+    reduce_start(1, residual[...], image_b[...], part_b, red_b)
+    image_out = pltpu.make_async_copy(image_b, image_hbm, out_sem.at[1])
+    image_out.start()
+
+    for it, win, cwins, own, red in (
+        (0, win_a, cwin_a, own_a, red_a),
+        (1, win_b, cwin_b, own_b, red_b),
     ):
         sent_pair(halo_copies(it, win))
         for level in range(1, top):
             sent_pair(coef_copies(it, level, cwins[level - 1]))
         for bit in range(bits):
             root_copy(it, bit, own).wait_send()
+        every_row(red, red_send.at[it]).wait()
+    residual_out.wait()
+    image_out.wait()
 
     beta = reduce_end(1, part_b, red_b)
-    sol_ref[...] = alpha * rhs[...] + beta * res_ref[...]
-    res_ref[...] = res_ref[...] - beta * image_b[...]
-
-    def drain(k, carry):
-        red_copy(0, k, part_a, red_a).wait_send()
-        red_copy(1, k, part_b, red_b).wait_send()
-        return carry
-
-    lax.fori_loop(1, count, drain, 0)
+    beta_ref[...] = jnp.broadcast_to(beta, beta_ref.shape)
 
 
 def body(
@@ -396,18 +421,23 @@
     top = len(sizes) - 1
     bits = root_couple.shape[1]
     root_couple = root_couple.reshape(root_couple.shape[1:])
-    smem = pl.BlockSpec(memory_space=pltpu.SMEM)
     hbm = pl.BlockSpec(memory_space=pl.ANY)
     vmem = pl.BlockSpec(memory_space=pltpu.VMEM)
     cwins = [pltpu.VMEM((3 * sizes[level], nrhs, rank), BF16) for level in range(1, top)]
     dma = pltpu.SemaphoreType.DMA
     out = jax.ShapeDtypeStruct(right_side.shape, F32)
-    return pl.pallas_call(
+    scalar = jax.ShapeDtypeStruct((nrhs, 128), F32)
+    residual, image, alpha, beta = pl.pallas_call(
         functools.partial(kernel, count),
-        out_shape=(out, out),
-        in_specs=[smem] * 5 + [hbm] * 6,
-        out_specs=(vmem, vmem),
+        out_shape=(out, out, scalar, scalar),
+        in_specs=[hbm] * 11,
+        out_specs=(hbm, hbm, vmem, vmem),
         scratch_shapes=[
+            pltpu.SMEM(near_source.shape[::-1], jnp.int32),
+            pltpu.SMEM(near_count.shape, jnp.int32),
+            pltpu.SMEM(couple_source.shape[::-1], jnp.int32),
+            pltpu.SMEM(couple_count.shape, jnp.int32),
+            pltpu.SMEM(root_mask.shape, jnp.int32),
             pltpu.VMEM(right_side.shape, F32),
             pltpu.VMEM(basis.shape, BF16),
             pltpu.VMEM(transfer.shape, BF16),
@@ -416,7 +446,8 @@
             pltpu.VMEM(root_couple.shape, BF16),
             pltpu.VMEM(right_side.shape, F32),
             pltpu.VMEM(right_side.shape, F32),
-            pltpu.VMEM((leaf_dev, nrhs, rank), BF16),
+            pltpu.VMEM(right_side.shape, F32),
+            pltpu.VMEM((couple.shape[0], nrhs, rank), F32),
             pltpu.VMEM((3 * leaf_dev, nrhs, leaf), BF16),
             pltpu.VMEM((3 * leaf_dev, nrhs, leaf), BF16),
             cwins,
@@ -427,16 +458,17 @@
             pltpu.VMEM((1, 128), F32),
             pltpu.VMEM((count, 1, 128), F32),
             pltpu.VMEM((count, 1, 128), F32),
-            dma((5,)),
+            dma((10,)),
             dma((leaf_dev,)),
+            dma((2,)),
             dma((2, 2)),
             dma((2, 2)),
             dma((2, top - 1, 2)),
             dma((2, top - 1, 2)),
             dma((2, bits)),
             dma((2, bits)),
-            dma((2, count)),
-            dma((2, count)),
+            dma((2,)),
+            dma((2,)),
         ],
         compiler_params=pltpu.CompilerParams(
             collective_id=0, has_side_effects=True, vmem_limit_bytes=56 << 20
@@ -459,6 +491,8 @@
         couple,
         root_couple,
     )
+    alpha, beta = alpha[:, :1], beta[:, :1]
+    return (alpha * right_side + beta * residual, residual - beta * image)
 
 
 def solution(mesh):

time: 40.5 us -> 34.7 us (0.86)
  Pallas kernels: 36.3 us -> 31 us
  local copies, waits for them, and re-layouts: 3.34 us -> 0.83 us
  other arithmetic: 0 us -> 1.94 us
    pallas_call x1, Pallas kernels: 36.3 us -> 31 us  [body(): pl.pallas_call(functools.partial(kernel, count), out_shape=(out, out, sca...]
    unnamed x2, local copies, waits for them, and re-layouts: 3.34 us -> 0.01 us
    sub x0 -> x1, other arithmetic: none -> 1.94 us  [body(): return (alpha * right_side + beta * residual, residual - beta * image)]
    slice x0 -> x1, local copies, waits for them, and re-layouts: none -> 0.83 us  [body(): alpha, beta = (alpha[:, :1], beta[:, :1])]
where the time goes in v1:
time: 34.7 us; the launch traced here: 34.4 us
  Pallas kernels  31 us (89%)
  other arithmetic  1.94 us (6%)
  local copies, waits for them, and re-layouts  0.83 us (2%)
  between operations  0.65 us (2%)
    pallas_call x1, Pallas kernels, body(): pl.pallas_call(functools.partial(kernel, count), out_shape=(out, out, sca...  31 us
    sub x1, other arithmetic, body(): return (alpha * right_side + beta * residual, residual - beta * image)  1.94 us
    slice x1, local copies, waits for them, and re-layouts, body(): alpha, beta = (alpha[:, :1], beta[:, :1])  0.83 us

profile of v1, /device:TPU:0, one launch (start us, length us, event | category | flops | bytes accessed | tf_op | source)
XLA Modules:
  0.0 34.4 jit_solution(9094072459791851317)
XLA Ops:
  0.6 0.0 copy-start
  0.6 31.0 %shard_map.122 = (f32[16,4096]{1,0:T(8,128)}, f32[16,4096]{1,0:T(8,128)}, f32[16,128]{1,0:T(8,128)}, f32[16,128]{1,0:T(8,128)}) custom-call(s32[8,16]{1,0:T(8,128)} %bitcast.4, s32[16]{0:T(128)} %near_count_hbm.1, s32[6,14]{1,0:T(8,128)} %bitcast.5, s32[14]{0:T(128)} %couple_count_hbm.1, s32[1,5]{1,0:T(1,128)} %root_mask_hbm.1, f32[16,4096]{1,0:T(8,128)} %rhs_hbm.1, ...), custom_call_target="tpu_custom_call" | custom-call | flops 536870912 | bytes 16777216 | tf_op jit(solution)/shard_map/pallas_call | solution.py:430
  31.6 0.8 %slice_reduce_fusion = (f32[16]{0:T(128)S(1)}, f32[16]{0:T(128)S(1)}) fusion(f32[16,128]{1,0:T(8,128)} %get-tuple-element.7, f32[16,128]{1,0:T(8,128)} %get-tuple-element.6), kind=kLoop, calls=%fused_computation.2 | loop fusion | bytes 256 | tf_op jit(solution)/shard_map/slice | solution.py:494
  32.5 0.0 copy-done
  32.5 1.9 %multiply_subtract_fusion = (f32[16,4096]{1,0:T(8,128)}, f32[16,4096]{1,0:T(8,128)}) fusion(f32[16,4096]{1,0:T(8,128)} %get-tuple-element.8, f32[16,4096]{1,0:T(8,128)} %get-tuple-element.9, f32[16]{0:T(128)S(1)} %get-tuple-element.12, f32[16,4096]{1,0:T(8,128)S(1)} %copy-done, f32[16]{0:T(128)S(1)} %get-tuple-element.13), kind=kLoop, calls=%fused_computation | loop fusion | flops 327680 | bytes 1310848 | tf_op jit(solution)/shard_map/sub | solution.py:495
Async XLA Ops:
  0.6 31.8 %copy-start = (f32[16,4096]{1,0:T(8,128)S(1)}, f32[16,4096]{1,0:T(8,128)}, u32[]{:S(2)}) copy-start(f32[16,4096]{1,0:T(8,128)} %rhs_hbm.1) | copy-start | bytes 786436

commit v2 on v1

--- a/solution.py
+++ b/solution.py
@@ -12,7 +12,7 @@
 BF16 = jnp.bfloat16
 SHRINK = 2.0**-10
 GROW = 2.0**10
-UNROLL = 4
+UNROLL = 8
 
 
 def dot(a, b):
@@ -399,6 +399,11 @@
 
     beta = reduce_end(1, part_b, red_b)
     beta_ref[...] = jnp.broadcast_to(beta, beta_ref.shape)
+
+
+def update(alpha, beta, rhs, residual, image, sol_ref, res_ref):
+    sol_ref[...] = alpha[:, :1] * rhs[...] + beta[:, :1] * residual[...]
+    res_ref[...] = residual[...] - beta[:, :1] * image[...]
 
 
 def body(
@@ -491,8 +496,12 @@
         couple,
         root_couple,
     )
-    alpha, beta = alpha[:, :1], beta[:, :1]
-    return (alpha * right_side + beta * residual, residual - beta * image)
+    return pl.pallas_call(
+        update,
+        out_shape=(out, out),
+        in_specs=[vmem] * 5,
+        out_specs=(vmem, vmem),
+    )(alpha, beta, right_side, residual, image)
 
 
 def solution(mesh):

time: 34.7 us -> 33.1 us (0.954)
  other arithmetic: 1.94 us -> 0 us
  Pallas kernels: 31 us -> 32.3 us
  local copies, waits for them, and re-layouts: 0.83 us -> 0 us
    pallas_call x0 -> x1, Pallas kernels: none -> 2.05 us  [body(): pl.pallas_call(update, out_shape=(out, out), in_specs=[vmem] * 5, out_spe...]
    sub x1 -> x0, other arithmetic: 1.94 us -> none  [body(): return (alpha * right_side + beta * residual, residual - beta * image)]
    slice x1 -> x0, local copies, waits for them, and re-layouts: 0.83 us -> none  [body(): alpha, beta = (alpha[:, :1], beta[:, :1])]
    pallas_call x1, Pallas kernels: 31 us -> 30.3 us  [body(): pl.pallas_call(functools.partial(kernel, count), out_shape=(out, out, sca...]
where the time goes in v2:
time: 33.1 us; the launch traced here: 33 us
  Pallas kernels  32.3 us (98%)
  between operations  0.64 us (2%)
    pallas_call x1, Pallas kernels, body(): pl.pallas_call(functools.partial(kernel, count), out_shape=(out, out, sca...  30.3 us
    pallas_call x1, Pallas kernels, body(): pl.pallas_call(update, out_shape=(out, out), in_specs=[vmem] * 5, out_spe...  2.05 us

profile of v2, /device:TPU:0, one launch (start us, length us, event | category | flops | bytes accessed | tf_op | source)
XLA Modules:
  0.0 33.0 jit_solution(5267664628176482558)
XLA Ops:
  0.6 30.3 %shard_map.122 = (f32[16,4096]{1,0:T(8,128)}, f32[16,4096]{1,0:T(8,128)}, f32[16,128]{1,0:T(8,128)}, f32[16,128]{1,0:T(8,128)}) custom-call(s32[8,16]{1,0:T(8,128)} %bitcast.4, s32[16]{0:T(128)} %near_count_hbm.1, s32[6,14]{1,0:T(8,128)} %bitcast.5, s32[14]{0:T(128)} %couple_count_hbm.1, s32[1,5]{1,0:T(1,128)} %root_mask_hbm.1, f32[16,4096]{1,0:T(8,128)} %rhs.1, ...), custom_call_target="tpu_custom_call" | custom-call | flops 536870912 | bytes 16777216 | tf_op jit(solution)/shard_map/pallas_call | solution.py:435
  30.9 2.0 %shard_map.123 = (f32[16,4096]{1,0:T(8,128)}, f32[16,4096]{1,0:T(8,128)}) custom-call(f32[16,128]{1,0:T(8,128)} %get-tuple-element.6.alpha, f32[16,128]{1,0:T(8,128)} %get-tuple-element.7.beta, f32[16,4096]{1,0:T(8,128)} %rhs.1, f32[16,4096]{1,0:T(8,128)} %get-tuple-element.8.residual, f32[16,4096]{1,0:T(8,128)} %get-tuple-element.9.image), custom_call_target="tpu_custom_call" | custom-call | tf_op jit(solution)/shard_map/pallas_call | solution.py:499
